TPU v7x, 32 devices: a whole 2x2x4 slice. The times are simulated.
32 devices in a mesh: ctx: 8 (over y, x, core), head: 4 (over z).
Axes of the slice: x: 2, y: 2, z: 4, core: 2. Of those that a mesh axis runs over, the one named last changes fastest.
Arguments:
- q_linear: bfloat16 [2048, 8192], P('ctx', 'head'), may hold values from -4 to 4
- k_linear: bfloat16 [2048, 8192], P('ctx', 'head'), may hold values from -4 to 4
- v_linear: bfloat16 [2048, 8192], P('ctx', 'head'), may hold values from -40 to 40
- log_decay: float32 [2048, 64], P('ctx', 'head'), may hold values from -1 to 0
- norm_gain: float32 [8192], P('head'), may hold values from 0.5 to 1.5
- q_soft: bfloat16 [2048, 8192], P('ctx', 'head'), may hold values from -6 to 6
- k_soft: bfloat16 [2048, 1024], P('ctx'), may hold values from -4 to 4
- v_soft: bfloat16 [2048, 1024], P('ctx'), may hold values from -4 to 4
Outputs:
- linear_out: bfloat16 [2048, 8192], P('ctx', 'head')
- soft_out: bfloat16 [2048, 8192], P('ctx', 'head')
All inputs are finite; a program needn't handle non-finite values.
Results may differ from a plain program's by a relative error of at most 0.0075.
Values may be sent and summed in bfloat16 or wider, within the bound.
A program may use at most 64 MiB of HBM per device.

v0:
```python
import jax
import jax.numpy as jnp
from jax import lax
from jax.sharding import PartitionSpec as P

QUERY_HEADS = 64
DH = 128
KV_HEADS = 8
BLOCK = 256


EPSILON = 1e-06
NEGATIVE = -1e30


def shifted(value, axis, steps):
    count = lax.axis_size(axis)
    first, last = (max(0, -steps), min(count, count - steps))
    return lax.ppermute(value, axis, [(source, source + steps) for source in range(first, last)])


def lightning_step(carry, inputs):
    running, log_before = carry
    queries, key_rows, value_rows, log_gates = inputs
    row_count = queries.shape[0]
    cumulative = jnp.cumsum(log_gates, axis=0)
    final_log = cumulative[-1]
    positions = jnp.arange(row_count, dtype=jnp.int32)
    causal = positions[None, :] <= positions[:, None]
    cum_heads = cumulative.T
    log_gap = jnp.where(causal[None], cum_heads[:, :, None] - cum_heads[:, None, :], NEGATIVE)
    scores = jnp.einsum("thd,shd->hts", queries, key_rows, preferred_element_type=jnp.float32)
    weights = (scores * jnp.exp(log_gap)).astype(jnp.bfloat16)
    intra_part = jnp.einsum("hts,she->the", weights, value_rows, preferred_element_type=jnp.float32)
    query_wide = queries.astype(jnp.float32)
    lifted_here = query_wide * jnp.exp(cumulative)[:, :, None]
    carried_here = jnp.einsum("thd,hde->the", lifted_here, running, precision=lax.Precision.HIGHEST)
    lifted_device = query_wide * jnp.exp(cumulative + log_before[None, :])[:, :, None]
    scaled = (key_rows * jnp.exp(final_log[None, :] - cumulative)[:, :, None]).astype(jnp.bfloat16)
    block_state = jnp.einsum("shd,she->hde", scaled, value_rows, preferred_element_type=jnp.float32)
    running = jnp.exp(final_log)[:, None, None] * running + block_state
    return ((running, log_before + final_log), (intra_part + carried_here, lifted_device))


def soft_update(running, queries, query_pos, key_rows, value_rows, key_pos):
    row_max, row_total, weighted = running
    head_count, row_count = row_max.shape
    kv_count, group_local = (queries.shape[1], queries.shape[2])
    scores = jnp.einsum("tkgd,skd->kgts", queries, key_rows, preferred_element_type=jnp.float32)
    scores = scores.reshape(head_count, row_count, key_rows.shape[0]) * DH ** (-0.5)
    allowed = key_pos[None, :] <= query_pos[:, None]
    scores = jnp.where(allowed[None], scores, NEGATIVE)
    new_max = jnp.maximum(row_max, jnp.max(scores, axis=2))
    probabilities = jnp.where(allowed[None], jnp.exp(scores - new_max[:, :, None]), 0.0)
    rescale = jnp.exp(row_max - new_max)
    row_total = row_total * rescale + jnp.sum(probabilities, axis=2)
    rounded = probabilities.astype(jnp.bfloat16).reshape(
        kv_count, group_local, row_count, key_rows.shape[0]
    )
    product = jnp.einsum(
        "kgts,ske->kgte", rounded, value_rows, preferred_element_type=jnp.float32
    ).reshape(head_count, row_count, DH)
    weighted = weighted * rescale[:, :, None] + product
    return (new_max, row_total, weighted)


def over_blocks(running, pieces, row_count, visitor):
    key_rows, value_rows = pieces

    def one_block(block_index, inner_state):
        block_start = block_index * row_count
        keys_here = lax.dynamic_slice_in_dim(key_rows, block_start, row_count, 0)
        values_here = lax.dynamic_slice_in_dim(value_rows, block_start, row_count, 0)
        return visitor(inner_state, keys_here, values_here, block_start)

    return lax.fori_loop(0, key_rows.shape[0] // row_count, one_block, running)


def finish(row_total, weighted, row_count, width):
    return (
        jnp.transpose(weighted / row_total[:, :, None], (1, 0, 2))
        .reshape(row_count, width)
        .astype(jnp.bfloat16)
    )


def local(q_linear, k_linear, v_linear, log_decay, norm_gain, q_soft, k_soft, v_soft):
    row_count = q_linear.shape[0]
    head_count = log_decay.shape[1]
    width = head_count * DH
    local_blocks = row_count // BLOCK
    lin_shape = (local_blocks, BLOCK, head_count, DH)
    sequences = (
        q_linear.reshape(lin_shape),
        k_linear.reshape(lin_shape),
        v_linear.reshape(lin_shape),
        log_decay.reshape(local_blocks, BLOCK, head_count),
    )
    start_carry = (
        jnp.zeros((head_count, DH, DH), jnp.float32),
        jnp.zeros((head_count,), jnp.float32),
    )
    (block_state, log_total), (local_part, lifted) = lax.scan(
        lightning_step, start_carry, sequences
    )
    local_part = local_part.reshape(row_count, head_count, DH)
    lifted = lifted.reshape(row_count, head_count, DH)
    block_fade = jnp.exp(log_total)

    def advance(step_index, entering):
        leaving = block_fade[:, None, None] * entering + block_state
        return shifted(leaving, "ctx", 1)

    entering = lax.fori_loop(0, lax.axis_size("ctx") - 1, advance, jnp.zeros_like(block_state))
    carried = jnp.einsum("thd,hde->the", lifted, entering, precision=lax.Precision.HIGHEST)
    mixed = (local_part + carried).reshape(row_count, width)
    power = lax.psum(jnp.sum(mixed * mixed, axis=1), "head") / (QUERY_HEADS * DH)
    linear_out = (mixed * lax.rsqrt(power + EPSILON)[:, None] * norm_gain[None, :]).astype(
        jnp.bfloat16
    )
    group_size = QUERY_HEADS // KV_HEADS
    kv_count = max(1, head_count // group_size)
    group_local = head_count // kv_count
    kv_start = lax.axis_index("head") * head_count // group_size
    k_local = lax.dynamic_slice_in_dim(k_soft, kv_start * DH, kv_count * DH, 1)
    v_local = lax.dynamic_slice_in_dim(v_soft, kv_start * DH, kv_count * DH, 1)
    query_shape = (row_count, kv_count, group_local, DH)
    key_shape = (row_count, kv_count, DH)
    my_index = lax.axis_index("ctx")
    positions = jnp.arange(row_count, dtype=jnp.int32)
    initial = (
        jnp.full((head_count, row_count), NEGATIVE, jnp.float32),
        jnp.zeros((head_count, row_count), jnp.float32),
        jnp.zeros((head_count, row_count, DH), jnp.float32),
    )
    queries = q_soft.reshape(query_shape)
    query_pos = my_index * row_count + positions
    query_end = my_index * row_count + row_count - 1

    def visitor(running, keys_here, values_here, block_start):
        return lax.cond(
            block_start <= query_end,
            lambda state: soft_update(
                state,
                queries,
                query_pos,
                keys_here.reshape(key_shape),
                values_here.reshape(key_shape),
                block_start + positions,
            ),
            lambda state: state,
            running,
        )

    row_max, row_total, weighted = over_blocks(
        initial,
        (
            lax.all_gather(k_local, "ctx", axis=0, tiled=True),
            lax.all_gather(v_local, "ctx", axis=0, tiled=True),
        ),
        row_count,
        visitor,
    )
    soft_out = finish(row_total, weighted, row_count, width)
    return (linear_out, soft_out)


def solution(mesh):
    return jax.shard_map(
        local,
        mesh=mesh,
        in_specs=(
            P("ctx", "head"),
            P("ctx", "head"),
            P("ctx", "head"),
            P("ctx", "head"),
            P("head"),
            P("ctx", "head"),
            P("ctx", None),
            P("ctx", None),
        ),
        out_specs=(P("ctx", "head"), P("ctx", "head")),
        check_vma=False,
    )
```

profile of v0, /device:TPU:6, one launch (start us, length us, event | category | flops | bytes accessed | tf_op | source)
XLA Modules:
  0.0 229.5 jit_solution(15106888393108270663)
XLA Ops:
  13.3 1.3 copy.54
  14.6 1.3 copy.67
  15.9 2.0 convolution_add_fusion
  18.0 126.6 %while.9 = (s32[]{:T(128)}, f32[16,128,128]{2,1,0:T(8,128)S(1)}, f32[16]{0:T(128)S(1)}, f32[16,128,128]{2,1,0:T(8,128)S(1)}, s32[]{:T(128)}) while((s32[]{:T(128)}, f32[16,128,128]{2,1,0:T(8,128)S(1)}, f32[16]{0:T(128)S(1)}, f32[16,128,128]{2,1,0:T(8,128)S(1)}, s32[]{:T(128)}) %tuple.84), condition=%wide.region_3.4_spmd, body=%wide.region_2.3_spmd.sunk | while | flops 524290 | bytes 7340197 | solution.py:114
  18.0 1.1 multiply_add_fusion.2
  19.2 1.9 collective-permute-start
  21.1 17.2 %collective-permute-done = f32[16,128,128]{2,1,0:T(8,128)S(1)} collective-permute-done((f32[16,128,128]{2,1,0:T(8,128)}, f32[16,128,128]{2,1,0:T(8,128)S(1)}, u32[]{:S(2)}, u32[]{:S(2)}) %collective-permute-start) | collective-permute-done | bytes 1048608 | tf_op jit(solution)/shard_map/while/body/eval_jaxpr/ppermute | solution.py:19
  39.4 1.9 collective-permute-start
  41.3 16.0 %collective-permute-done = f32[16,128,128]{2,1,0:T(8,128)S(1)} collective-permute-done((f32[16,128,128]{2,1,0:T(8,128)}, f32[16,128,128]{2,1,0:T(8,128)S(1)}, u32[]{:S(2)}, u32[]{:S(2)}) %collective-permute-start) | collective-permute-done | bytes 1048608 | tf_op jit(solution)/shard_map/while/body/eval_jaxpr/ppermute | solution.py:19
  58.4 1.9 collective-permute-start
  60.4 14.4 %collective-permute-done = f32[16,128,128]{2,1,0:T(8,128)S(1)} collective-permute-done((f32[16,128,128]{2,1,0:T(8,128)}, f32[16,128,128]{2,1,0:T(8,128)S(1)}, u32[]{:S(2)}, u32[]{:S(2)}) %collective-permute-start) | collective-permute-done | bytes 1048608 | tf_op jit(solution)/shard_map/while/body/eval_jaxpr/ppermute | solution.py:19
  75.9 1.9 collective-permute-start
  77.8 14.4 %collective-permute-done = f32[16,128,128]{2,1,0:T(8,128)S(1)} collective-permute-done((f32[16,128,128]{2,1,0:T(8,128)}, f32[16,128,128]{2,1,0:T(8,128)S(1)}, u32[]{:S(2)}, u32[]{:S(2)}) %collective-permute-start) | collective-permute-done | bytes 1048608 | tf_op jit(solution)/shard_map/while/body/eval_jaxpr/ppermute | solution.py:19
  93.4 1.9 collective-permute-start
  95.3 14.4 %collective-permute-done = f32[16,128,128]{2,1,0:T(8,128)S(1)} collective-permute-done((f32[16,128,128]{2,1,0:T(8,128)}, f32[16,128,128]{2,1,0:T(8,128)S(1)}, u32[]{:S(2)}, u32[]{:S(2)}) %collective-permute-start) | collective-permute-done | bytes 1048608 | tf_op jit(solution)/shard_map/while/body/eval_jaxpr/ppermute | solution.py:19
  110.8 1.9 collective-permute-start
  112.7 14.4 %collective-permute-done = f32[16,128,128]{2,1,0:T(8,128)S(1)} collective-permute-done((f32[16,128,128]{2,1,0:T(8,128)}, f32[16,128,128]{2,1,0:T(8,128)S(1)}, u32[]{:S(2)}, u32[]{:S(2)}) %collective-permute-start) | collective-permute-done | bytes 1048608 | tf_op jit(solution)/shard_map/while/body/eval_jaxpr/ppermute | solution.py:19
  128.3 1.9 collective-permute-start
  130.2 14.4 %collective-permute-done = f32[16,128,128]{2,1,0:T(8,128)S(1)} collective-permute-done((f32[16,128,128]{2,1,0:T(8,128)}, f32[16,128,128]{2,1,0:T(8,128)S(1)}, u32[]{:S(2)}, u32[]{:S(2)}) %collective-permute-start) | collective-permute-done | bytes 1048608 | tf_op jit(solution)/shard_map/while/body/eval_jaxpr/ppermute | solution.py:19
  144.6 3.7 %fusion.17 = f32[16,128,256]{2,1,0:T(8,128)} fusion(f32[16,128,128]{2,1,0:T(8,128)S(1)} %get-tuple-element.343, f32[256,16]{0,1:T(8,128)S(1)} %get-tuple-element.428, bf16[256,2048]{1,0:T(8,128)(2,1)S(1)} %copy-done), kind=kOutput, calls=%fused_computation.34 | convolution fusion | flops 806354944 | bytes 4210688 | tf_op jit(solution)/shard_map/thd,hde->the/dot_general | solution.py:115
  148.3 4.8 %fusion.19 = f32[16,256,128]{1,2,0:T(8,128)} fusion(bf16[256,16,128]{0,2,1:T(8,128)(2,1)} %bitcast.116, f32[16,256]{1,0:T(8,128)S(1)} %get-tuple-element.426, pred[256,256]{1,0:T(8,128)(4,1)S(1)} %iota_compare_fusion, bf16[256,2048]{1,0:T(8,128)(2,1)} %param.16, bf16[256,2048]{1,0:T(8,128)(2,1)S(1)} %copy-done), kind=kOutput, calls=%fused_computation.36 | convolution fusion | flops 541065216 | bytes 5324800 | tf_op jit(solution)/shard_map/while/body/eval_jaxpr/hts,she->the/dot_general | solution.py:34
  153.1 4.7 %multiply_reduce_fusion = (f32[256]{0:T(256)S(1)}, f32[256,16,128]{0,2,1:T(8,128)}) fusion(f32[16,128,256]{2,1,0:T(8,128)S(1)} %copy-done.1, f32[256,16]{0,1:T(8,128)S(1)} %get-tuple-element.428, f32[16,256,128]{1,2,0:T(8,128)} %fusion.19, bf16[256,2048]{1,0:T(8,128)(2,1)S(1)} %copy-done), kind=kOutput, calls=%fused_computation.31 | convolution fusion | flops 808451840 | bytes 7357440 | tf_op jit(solution)/shard_map/while/body/eval_jaxpr/thd,hde->the/dot_general | solution.py:37
  157.8 1.9 copy.50
  159.8 12.7 %psum.7 = f32[256]{0:T(256)S(1)} all-reduce(f32[256]{0:T(256)S(1)} %get-tuple-element.432), channel_id=1, replica_groups=mesh['ctx'=8,'head'=4] {'head'}, use_global_device_ids=true, to_apply=%region_5.6 | all-reduce | flops 256 | bytes 2048 | tf_op jit(solution)/shard_map/psum | solution.py:117
  172.5 1.2 multiply_convert_fusion.1
  173.9 47.2 %while.36 = (s32[]{:T(128)}, f32[16,256]{1,0:T(8,128)S(1)}, f32[16,256]{1,0:T(8,128)S(1)}, f32[16,256,128]{2,1,0:T(8,128)S(1)}, s32[]{:T(128)}, /*index=5*/bf16[...) while((s32[]{:T(128)}, f32[16,256]{1,0:T(8,128)S(1)}, ...), condition=%wide.region_11.12_spmd.clone, body=%wide.region_6.11_spmd.clone.sunk | while | flops 551625216 | bytes 23338300 | solution.py:76
  173.9 6.7 %conditional.3 = ((f32[16,256]{1,0:T(8,128)S(1)}, f32[16,256]{1,0:T(8,128)S(1)}, f32[16,256,128]{2,1,0:T(8,128)S(1)})) conditional(s32[]{:T(128)} %convert_element_type.74, (f32[16,256]{1,0:T(8,128)S(1)}, f32[16,256]{1,0:T(8,128)S(1)}, f32[16,256,128]{2,1,0:T(8,128)S(1)}) %tuple.80, (s32[]{:T(128)}, s32[256]{0:T(256)S(1)}, s32[]{:T(128)}, ...), branch_computations={%region_7.7_spmd, %region_8.10_spmd} | conditional | flops 551625216 | bytes 23337038 | solution.py:141
  175.1 2.1 fusion.4
  177.2 1.4 fusion.7
  180.7 6.7 %conditional.3 = ((f32[16,256]{1,0:T(8,128)S(1)}, f32[16,256]{1,0:T(8,128)S(1)}, f32[16,256,128]{2,1,0:T(8,128)S(1)})) conditional(s32[]{:T(128)} %convert_element_type.74, (f32[16,256]{1,0:T(8,128)S(1)}, f32[16,256]{1,0:T(8,128)S(1)}, f32[16,256,128]{2,1,0:T(8,128)S(1)}) %tuple.80, (s32[]{:T(128)}, s32[256]{0:T(256)S(1)}, s32[]{:T(128)}, ...), branch_computations={%region_7.7_spmd, %region_8.10_spmd} | conditional | flops 551625216 | bytes 23337038 | solution.py:141
  181.8 2.1 fusion.4
  183.9 1.4 fusion.7
  187.4 6.7 %conditional.3 = ((f32[16,256]{1,0:T(8,128)S(1)}, f32[16,256]{1,0:T(8,128)S(1)}, f32[16,256,128]{2,1,0:T(8,128)S(1)})) conditional(s32[]{:T(128)} %convert_element_type.74, (f32[16,256]{1,0:T(8,128)S(1)}, f32[16,256]{1,0:T(8,128)S(1)}, f32[16,256,128]{2,1,0:T(8,128)S(1)}) %tuple.80, (s32[]{:T(128)}, s32[256]{0:T(256)S(1)}, s32[]{:T(128)}, ...), branch_computations={%region_7.7_spmd, %region_8.10_spmd} | conditional | flops 551625216 | bytes 23337038 | solution.py:141
  188.6 2.1 fusion.4
  190.7 1.4 fusion.7
  194.1 6.7 %conditional.3 = ((f32[16,256]{1,0:T(8,128)S(1)}, f32[16,256]{1,0:T(8,128)S(1)}, f32[16,256,128]{2,1,0:T(8,128)S(1)})) conditional(s32[]{:T(128)} %convert_element_type.74, (f32[16,256]{1,0:T(8,128)S(1)}, f32[16,256]{1,0:T(8,128)S(1)}, f32[16,256,128]{2,1,0:T(8,128)S(1)}) %tuple.80, (s32[]{:T(128)}, s32[256]{0:T(256)S(1)}, s32[]{:T(128)}, ...), branch_computations={%region_7.7_spmd, %region_8.10_spmd} | conditional | flops 551625216 | bytes 23337038 | solution.py:141
  195.3 2.1 fusion.4
  197.4 1.4 fusion.7
  200.9 6.7 %conditional.3 = ((f32[16,256]{1,0:T(8,128)S(1)}, f32[16,256]{1,0:T(8,128)S(1)}, f32[16,256,128]{2,1,0:T(8,128)S(1)})) conditional(s32[]{:T(128)} %convert_element_type.74, (f32[16,256]{1,0:T(8,128)S(1)}, f32[16,256]{1,0:T(8,128)S(1)}, f32[16,256,128]{2,1,0:T(8,128)S(1)}) %tuple.80, (s32[]{:T(128)}, s32[256]{0:T(256)S(1)}, s32[]{:T(128)}, ...), branch_computations={%region_7.7_spmd, %region_8.10_spmd} | conditional | flops 551625216 | bytes 23337038 | solution.py:141
  202.0 2.1 fusion.4
  204.1 1.4 fusion.7
  207.6 6.7 %conditional.3 = ((f32[16,256]{1,0:T(8,128)S(1)}, f32[16,256]{1,0:T(8,128)S(1)}, f32[16,256,128]{2,1,0:T(8,128)S(1)})) conditional(s32[]{:T(128)} %convert_element_type.74, (f32[16,256]{1,0:T(8,128)S(1)}, f32[16,256]{1,0:T(8,128)S(1)}, f32[16,256,128]{2,1,0:T(8,128)S(1)}) %tuple.80, (s32[]{:T(128)}, s32[256]{0:T(256)S(1)}, s32[]{:T(128)}, ...), branch_computations={%region_7.7_spmd, %region_8.10_spmd} | conditional | flops 551625216 | bytes 23337038 | solution.py:141
  208.8 2.1 fusion.4
  210.9 1.4 fusion.7
  214.3 6.7 %conditional.3 = ((f32[16,256]{1,0:T(8,128)S(1)}, f32[16,256]{1,0:T(8,128)S(1)}, f32[16,256,128]{2,1,0:T(8,128)S(1)})) conditional(s32[]{:T(128)} %convert_element_type.74, (f32[16,256]{1,0:T(8,128)S(1)}, f32[16,256]{1,0:T(8,128)S(1)}, f32[16,256,128]{2,1,0:T(8,128)S(1)}) %tuple.80, (s32[]{:T(128)}, s32[256]{0:T(256)S(1)}, s32[]{:T(128)}, ...), branch_computations={%region_7.7_spmd, %region_8.10_spmd} | conditional | flops 551625216 | bytes 23337038 | solution.py:141
  215.5 2.1 fusion.4
  217.6 1.4 fusion.7
  221.1 1.5 copy_bitcast_fusion
  (107 shorter events, 35.0 us)
Async XLA Ops:
  7.2 137.4 %copy-start = (bf16[256,2048]{1,0:T(8,128)(2,1)S(1)}, bf16[256,2048]{1,0:T(8,128)(2,1)}, u32[]{:S(2)}) copy-start(bf16[256,2048]{1,0:T(8,128)(2,1)} %param.14) | copy-start | bytes 3145732
  7.2 5.6 %copy-start.2 = (bf16[256,2048]{1,0:T(8,128)(2,1)S(1)}, bf16[256,2048]{1,0:T(8,128)(2,1)}, u32[]{:S(2)}) copy-start(bf16[256,2048]{1,0:T(8,128)(2,1)} %param.19) | copy-start | bytes 3145732
  7.2 166.5 %all-gather.3.cloned.1.call-start = ((), (), s32[]{:S(2)}) async-start(), calls=%async_computation | async-start | bytes 1179648 | tf_op jit(solution)/shard_map/all_gather | solution.py:158
  9.1 164.6 %all-gather.5.cloned.1.call-start = ((), (), s32[]{:S(2)}) async-start(), calls=%async_computation.1 | async-start | bytes 1179648 | tf_op jit(solution)/shard_map/all_gather | solution.py:159
  13.3 1.3 copy-start.3
  19.2 19.1 %collective-permute-start = (f32[16,128,128]{2,1,0:T(8,128)}, f32[16,128,128]{2,1,0:T(8,128)S(1)}, u32[]{:S(2)}, u32[]{:S(2)}) collective-permute-start(f32[16,128,128]{2,1,0:T(8,128)} %multiply_add_fusion.2), channel_id=1, source_target_pairs={{0,4},{4,8},{8,12},{12,16},{16,20},{20,24},{24,28},{1,5},{5,9},{9,... | collective-permute-start | bytes 3145736 | tf_op jit(solution)/shard_map/while/body/eval_jaxpr/ppermute | solution.py:19
  39.4 17.9 %collective-permute-start = (f32[16,128,128]{2,1,0:T(8,128)}, f32[16,128,128]{2,1,0:T(8,128)S(1)}, u32[]{:S(2)}, u32[]{:S(2)}) collective-permute-start(f32[16,128,128]{2,1,0:T(8,128)} %multiply_add_fusion.2), channel_id=1, source_target_pairs={{0,4},{4,8},{8,12},{12,16},{16,20},{20,24},{24,28},{1,5},{5,9},{9,... | collective-permute-start | bytes 3145736 | tf_op jit(solution)/shard_map/while/body/eval_jaxpr/ppermute | solution.py:19
  58.4 16.3 %collective-permute-start = (f32[16,128,128]{2,1,0:T(8,128)}, f32[16,128,128]{2,1,0:T(8,128)S(1)}, u32[]{:S(2)}, u32[]{:S(2)}) collective-permute-start(f32[16,128,128]{2,1,0:T(8,128)} %multiply_add_fusion.2), channel_id=1, source_target_pairs={{0,4},{4,8},{8,12},{12,16},{16,20},{20,24},{24,28},{1,5},{5,9},{9,... | collective-permute-start | bytes 3145736 | tf_op jit(solution)/shard_map/while/body/eval_jaxpr/ppermute | solution.py:19
  75.9 16.3 %collective-permute-start = (f32[16,128,128]{2,1,0:T(8,128)}, f32[16,128,128]{2,1,0:T(8,128)S(1)}, u32[]{:S(2)}, u32[]{:S(2)}) collective-permute-start(f32[16,128,128]{2,1,0:T(8,128)} %multiply_add_fusion.2), channel_id=1, source_target_pairs={{0,4},{4,8},{8,12},{12,16},{16,20},{20,24},{24,28},{1,5},{5,9},{9,... | collective-permute-start | bytes 3145736 | tf_op jit(solution)/shard_map/while/body/eval_jaxpr/ppermute | solution.py:19
  93.4 16.3 %collective-permute-start = (f32[16,128,128]{2,1,0:T(8,128)}, f32[16,128,128]{2,1,0:T(8,128)S(1)}, u32[]{:S(2)}, u32[]{:S(2)}) collective-permute-start(f32[16,128,128]{2,1,0:T(8,128)} %multiply_add_fusion.2), channel_id=1, source_target_pairs={{0,4},{4,8},{8,12},{12,16},{16,20},{20,24},{24,28},{1,5},{5,9},{9,... | collective-permute-start | bytes 3145736 | tf_op jit(solution)/shard_map/while/body/eval_jaxpr/ppermute | solution.py:19
  110.8 16.3 %collective-permute-start = (f32[16,128,128]{2,1,0:T(8,128)}, f32[16,128,128]{2,1,0:T(8,128)S(1)}, u32[]{:S(2)}, u32[]{:S(2)}) collective-permute-start(f32[16,128,128]{2,1,0:T(8,128)} %multiply_add_fusion.2), channel_id=1, source_target_pairs={{0,4},{4,8},{8,12},{12,16},{16,20},{20,24},{24,28},{1,5},{5,9},{9,... | collective-permute-start | bytes 3145736 | tf_op jit(solution)/shard_map/while/body/eval_jaxpr/ppermute | solution.py:19
  128.3 16.3 %collective-permute-start = (f32[16,128,128]{2,1,0:T(8,128)}, f32[16,128,128]{2,1,0:T(8,128)S(1)}, u32[]{:S(2)}, u32[]{:S(2)}) collective-permute-start(f32[16,128,128]{2,1,0:T(8,128)} %multiply_add_fusion.2), channel_id=1, source_target_pairs={{0,4},{4,8},{8,12},{12,16},{16,20},{20,24},{24,28},{1,5},{5,9},{9,... | collective-permute-start | bytes 3145736 | tf_op jit(solution)/shard_map/while/body/eval_jaxpr/ppermute | solution.py:19
  148.3 4.8 %copy-start.1 = (f32[16,128,256]{2,1,0:T(8,128)S(1)}, f32[16,128,256]{2,1,0:T(8,128)}, u32[]{:S(2)}) copy-start(f32[16,128,256]{2,1,0:T(8,128)} %fusion.17) | copy-start | bytes 6291460
  157.8 14.6 %copy-start.4 = (f32[2048]{0:T(1024)S(1)}, f32[2048]{0:T(1024)}, u32[]{:S(2)}) copy-start(f32[2048]{0:T(1024)} %param.18) | copy-start | bytes 24580
Sparse Core Ops, SparseCore 0:
  9.9 25.1 all-gather.2
  37.0 24.8 all-gather.4
where the time goes:
time: 230 us; the launch traced here: 229 us
  waiting for transfers between devices  105 us (46%)
  matrix products  39.6 us (17%)
  other arithmetic  26.4 us (11%)
  local copies, waits for them, and re-layouts  16.9 us (7%)
  between operations  14.2 us (6%)
  starting transfers between devices  13.4 us (6%)
  blocking collectives  12.7 us (6%)
    ppermute x7, waiting for transfers between devices, shifted(): lax.ppermute(value, axis, [(source, source + steps) for source in range(f...  105 us
    dot_general x7, matrix products, soft_update(): jnp.einsum('tkgd,skd->kgts', queries, key_rows, preferred_element_type=jn...  14.6 us
    ppermute x7, starting transfers between devices, shifted(): lax.ppermute(value, axis, [(source, source + steps) for source in range(f...  13.4 us
    psum x1, blocking collectives, local(): lax.psum(jnp.sum(mixed * mixed, axis=1), 'head') / (QUERY_HEADS * DH)  12.7 us
    dot_general x7, matrix products, soft_update(): jnp.einsum('kgts,ske->kgte', rounded, value_rows, preferred_element_type=...  9.76 us
    add x7, other arithmetic, advance(): leaving = block_fade[:, None, None] * entering + block_state  7.96 us
    reduce_sum x7, other arithmetic, soft_update(): row_total = row_total * rescale + jnp.sum(probabilities, axis=2)  7.15 us
    dynamic_slice x7, local copies, waits for them, and re-layouts, one_block(): lax.dynamic_slice_in_dim(value_rows, block_start, row_count, 0)  6.95 us
  transfers between devices with their start and end apart: 9, of which 7 were waited for; matrix products, arithmetic and copies ran while one was open for 14% of the time, Pallas kernels for 0%

commit v1 on v0

v1 whole, which is shorter than its diff:
```python
import functools

import jax
import jax.numpy as jnp
from jax import lax
from jax.experimental import pallas as pl
from jax.experimental.pallas import tpu as pltpu
from jax.sharding import PartitionSpec as P

QUERY_HEADS = 64
DH = 128
KV_HEADS = 8
EPSILON = 1e-06
NEGATIVE = -1e30
LOG2E = 1.4426950408889634
MESH = pl.DeviceIdType.MESH
F32 = jnp.float32
BF16 = jnp.bfloat16
HIGHEST = lax.Precision.HIGHEST


def mm(a, b, ca, cb, precision=None):
    return lax.dot_general(
        a, b, (((ca,), (cb,)), ((), ())), preferred_element_type=F32, precision=precision
    )


def cols(index):
    return pl.ds(pl.multiple_of(index * DH, DH), DH)


def kernel(
    n, zn, heads, kvc, ch,
    ld_ref, gain_ref, ql_hbm, kl_hbm, vl_hbm, qs_hbm, ks_hbm, vs_hbm,
    lin_hbm, soft_hbm,
    ql, kl, vl, qs, kv, lin, soft, cumc, cumr, state, mixed, ein, eout, mx, tot, acc, pw,
    in_sem, own_sem, out_sem, kv_recv, dir_send, sib_send, rel_send, ch_send, ch_recv, pw_send, pw_recv,
):
    c = lax.axis_index("ctx")
    z = lax.axis_index("head")
    rows = ql.shape[0]
    chips = n // 2
    chip, core = c // 2, c % 2
    sib = chip * 2 + 1 - core
    group = heads // kvc
    chunks = heads // ch

    start = pl.multiple_of((z * heads // (QUERY_HEADS // KV_HEADS)) * DH, DH)
    own = [
        pltpu.make_async_copy(src.at[:, pl.ds(start, kvc * DH)], kv.at[c, i], own_sem.at[i])
        for i, src in enumerate((ks_hbm, vs_hbm))
    ]
    loads = [
        pltpu.make_async_copy(src, dst, in_sem.at[i])
        for i, (src, dst) in enumerate(((kl_hbm, kl), (vl_hbm, vl), (ql_hbm, ql), (qs_hbm, qs)))
    ]
    for copy in own + loads:
        copy.start()

    barrier = pltpu.get_barrier_semaphore()
    for d in range(1, n):
        pl.semaphore_signal(barrier, inc=1, device_id={"ctx": lax.rem(c + d, n)}, device_id_type=MESH)
    for d in range(1, zn):
        pl.semaphore_signal(barrier, inc=1, device_id={"head": lax.rem(z + d, zn)}, device_id_type=MESH)
    pl.semaphore_wait(barrier, n - 1 + zn - 1)

    def kv_copy(block, i, send, target):
        return pltpu.make_async_remote_copy(
            src_ref=kv.at[block, i], dst_ref=kv.at[block, i],
            send_sem=send, recv_sem=kv_recv.at[block, i],
            device_id={"ctx": target}, device_id_type=MESH,
        )

    def direct(i, to):
        return kv_copy(c, i, dir_send.at[to, i], to * 2 + core)

    def sibling(i):
        return kv_copy(c, i, sib_send.at[i], sib)

    def relayed(i, source):
        return kv_copy(source * 2 + core, i, rel_send.at[source, i], sib)

    def arrived(block, i):
        kv_copy(block, i, sib_send.at[i], sib).wait_recv()

    for copy in own:
        copy.wait()

    @pl.when(core == 0)
    def _():
        for i in range(2):
            sibling(i).start()

    def send_direct(to, _):
        for i in range(2):
            direct(i, to).start()
        return 0

    lax.fori_loop(chip + 1, chips, send_direct, 0)

    row_id = lax.broadcasted_iota(jnp.int32, (rows, rows), 0)
    col_id = lax.broadcasted_iota(jnp.int32, (rows, rows), 1)
    tri = jnp.where(col_id <= row_id, 1.0, 0.0).astype(F32)
    ld = ld_ref[...]
    cum = mm(tri, ld, 1, 0, HIGHEST)
    cumr[...] = cum.T
    for h in range(heads):
        cumc[h] = jnp.broadcast_to(cum[:, h : h + 1], (rows, DH))
    for copy in loads[:2]:
        copy.wait()

    def states(h):
        cc = cumc[h]
        last = cc[rows - 1 : rows, :]
        decayed = (kl[:, cols(h)].astype(F32) * jnp.exp(last - cc)).astype(BF16)
        state[h] = mm(decayed, vl[:, cols(h)], 0, 0)

    def over_heads(body, count, unroll):
        unroll = min(unroll, count)

        def step(j, _):
            for u in range(unroll):
                body(j * unroll + u)
            return 0

        lax.fori_loop(0, count // unroll, step, 0)

    over_heads(states, heads, 4)
    for copy in loads[2:]:
        copy.wait()

    def intra(h):
        raw = mm(ql[:, cols(h)], kl[:, cols(h)], 1, 1)
        cc = cumc[h]
        gap = jnp.concatenate([cc] * (rows // DH), axis=1) - cumr[pl.ds(h, 1), :]
        r = lax.broadcasted_iota(jnp.int32, (rows, rows), 0)
        s = lax.broadcasted_iota(jnp.int32, (rows, rows), 1)
        w = (raw * jnp.exp(jnp.where(s <= r, gap, NEGATIVE))).astype(BF16)
        mixed[h] = mm(w, vl[:, cols(h)], 1, 0)

    def chain_copy(j):
        return pltpu.make_async_remote_copy(
            src_ref=eout.at[pl.ds(j * ch, ch)], dst_ref=ein.at[pl.ds(j * ch, ch)],
            send_sem=ch_send.at[j], recv_sem=ch_recv.at[j],
            device_id={"ctx": jnp.minimum(c + 1, n - 1)}, device_id_type=MESH,
        )

    def first_chain():
        def step(j, _):
            part = pl.ds(j * ch, ch)
            eout[part] = state[part].astype(BF16)
            chain_copy(j).start()
            return 0

        lax.fori_loop(0, chunks, step, 0)

    def chain():
        def step(j, _):
            chain_copy(j).wait_recv()

            @pl.when(c < n - 1)
            def _():
                for u in range(ch):
                    h = j * ch + u
                    fade = jnp.exp(cumc[h, rows - 1 : rows, :])
                    eout[h] = (fade * ein[h].astype(F32) + state[h]).astype(BF16)
                chain_copy(j).start()

            for u in range(ch):
                h = j * ch + u
                carried = mm(ql[:, cols(h)], ein[h], 1, 0)
                mixed[h] = mixed[h] + carried * jnp.exp(cumc[h])
            return 0

        lax.fori_loop(0, chunks, step, 0)

    def power_copy(d):
        return pltpu.make_async_remote_copy(
            src_ref=pw.at[0], dst_ref=pw.at[zn - d],
            send_sem=pw_send.at[d], recv_sem=pw_recv.at[zn - d],
            device_id={"head": lax.rem(z + d, zn)}, device_id_type=MESH,
        )

    def power():
        def step(h, total):
            m = mixed[h]
            return total + m * m

        part = lax.fori_loop(0, heads, step, jnp.zeros((rows, DH), F32))
        pw[0] = mm(jnp.ones((8, DH), F32), part, 1, 1, HIGHEST)
        for d in range(1, zn):
            power_copy(d).start()

    scale = DH ** (-0.5) * LOG2E

    def group_dot(h, keys):
        return mm(qs[:, cols(h)], keys, 1, 1) * scale

    def soft_own():
        for g in range(kvc):
            keys = kv[c, 0, :, g * DH : (g + 1) * DH]
            values = kv[c, 1, :, g * DH : (g + 1) * DH]

            def one(u):
                h = g * group + u
                s = group_dot(h, keys)
                r = lax.broadcasted_iota(jnp.int32, (rows, rows), 0)
                t = lax.broadcasted_iota(jnp.int32, (rows, rows), 1)
                s = jnp.where(t <= r, s, NEGATIVE)
                top = jnp.max(s, axis=1, keepdims=True)
                p = jnp.exp2(s - top)
                mx[h] = jnp.broadcast_to(top, (rows, DH))
                tot[h] = sum(p[:, i : i + DH] for i in range(0, rows, DH))
                acc[h] = mm(p.astype(BF16), values, 1, 0)

            over_heads(one, group, 4)

    def soft_full(first, count):
        for g in range(kvc):
            part = slice(g * DH, (g + 1) * DH)
            keys = kv[pl.ds(first, count), 0, :, part].reshape(count * rows, DH)
            values = kv[pl.ds(first, count), 1, :, part].reshape(count * rows, DH)

            def one(u):
                h = g * group + u
                s = group_dot(h, keys)
                before = mx[h]
                top = jnp.maximum(before, jnp.max(s, axis=1, keepdims=True))
                fade = jnp.exp2(before - top)
                p = [jnp.exp2(s[:, i : i + DH] - top) for i in range(0, count * rows, DH)]
                mx[h] = top
                tot[h] = tot[h] * fade + sum(p)
                packed = jnp.concatenate([x.astype(BF16) for x in p], axis=1)
                acc[h] = acc[h] * fade + mm(packed, values, 1, 0)

            over_heads(one, group, 4)

    def relay(source):
        for i in range(2):
            arrived(source * 2 + core, i)
            relayed(i, source).start()

    def pair(source):
        for i in range(2):
            arrived(source * 2 + 1 - core, i)
        soft_full(source * 2, 2)

    @pl.when(c == 0)
    def _():
        first_chain()

    over_heads(intra, heads, 2)

    @pl.when(chip > 0)
    def _():
        relay(chip - 1)

    @pl.when(c == 0)
    def _():
        power()

    @pl.when(c == 1)
    def _():
        chain()
        power()

    soft_own()

    @pl.when(core == 1)
    def _():
        for i in range(2):
            arrived(c - 1, i)
        soft_full(c - 1, 1)

    @pl.when(chip > 0)
    def _():
        def step(k, _):
            source = chip - 1 - k

            @pl.when(source == 0)
            def _():
                chain()
                power()

            @pl.when(source > 0)
            def _():
                relay(source - 1)

            pair(source)
            return 0

        lax.fori_loop(0, chip, step, 0)

    def soft_end(h):
        total = jnp.sum(tot[h], axis=1, keepdims=True)
        soft[:, cols(h)] = (acc[h] / total).astype(BF16)

    over_heads(soft_end, heads, 2)
    soft_out = pltpu.make_async_copy(soft, soft_hbm, out_sem.at[0])
    soft_out.start()

    for d in range(1, zn):
        power_copy(d).wait_recv()
    squares = pw[0]
    for d in range(1, zn):
        squares = squares + pw[d]
    mean = mm(squares, jnp.full((8, DH), 0.125, F32), 0, 0, HIGHEST) / (QUERY_HEADS * DH)
    norm = lax.rsqrt(mean + EPSILON)

    def lin_end(h):
        lin[:, cols(h)] = (mixed[h] * norm * gain_ref[pl.ds(h, 1), :]).astype(BF16)

    over_heads(lin_end, heads, 2)
    lin_out = pltpu.make_async_copy(lin, lin_hbm, out_sem.at[1])
    lin_out.start()

    for d in range(1, zn):
        power_copy(d).wait_send()

    @pl.when(c < n - 1)
    def _():
        lax.fori_loop(0, chunks, lambda j, _: (chain_copy(j).wait_send(), 0)[1], 0)

    @pl.when(core == 0)
    def _():
        for i in range(2):
            sibling(i).wait_send()

    def sent_direct(to, _):
        for i in range(2):
            direct(i, to).wait_send()
        return 0

    lax.fori_loop(chip + 1, chips, sent_direct, 0)

    def sent_relay(source, _):
        for i in range(2):
            relayed(i, source).wait_send()
        return 0

    lax.fori_loop(0, chip, sent_relay, 0)
    soft_out.wait()
    lin_out.wait()


def local(n, zn, q_linear, k_linear, v_linear, log_decay, norm_gain, q_soft, k_soft, v_soft):
    rows, width = q_linear.shape
    heads = width // DH
    kvc = max(1, heads // (QUERY_HEADS // KV_HEADS))
    ch = 2
    anywhere = pl.BlockSpec(memory_space=pl.ANY)
    whole = pl.BlockSpec(memory_space=pltpu.VMEM)
    dma = pltpu.SemaphoreType.DMA
    chips = n // 2
    chunks = heads // ch
    out = jax.ShapeDtypeStruct((rows, width), BF16)
    wide = pltpu.VMEM((rows, width), BF16)
    per_head = pltpu.VMEM((heads, rows, DH), F32)
    return pl.pallas_call(
        functools.partial(kernel, n, zn, heads, kvc, ch),
        out_shape=(out, out),
        in_specs=[whole, whole] + [anywhere] * 6,
        out_specs=(anywhere, anywhere),
        scratch_shapes=[
            wide, wide, wide, wide,
            pltpu.VMEM((n, 2, rows, kvc * DH), BF16),
            wide, wide,
            per_head,
            pltpu.VMEM((heads, rows), F32),
            pltpu.VMEM((heads, DH, DH), F32),
            per_head,
            pltpu.VMEM((heads, DH, DH), BF16),
            pltpu.VMEM((heads, DH, DH), BF16),
            per_head, per_head, per_head,
            pltpu.VMEM((zn, 8, rows), F32),
            dma((4,)), dma((2,)), dma((2,)),
            dma((n, 2)), dma((chips, 2)), dma((2,)), dma((chips, 2)),
            dma((chunks,)), dma((chunks,)), dma((zn,)), dma((zn,)),
        ],
        compiler_params=pltpu.CompilerParams(
            collective_id=0, has_side_effects=True, vmem_limit_bytes=56 * 2**20
        ),
    )(log_decay, norm_gain.reshape(heads, DH), q_linear, k_linear, v_linear, q_soft, k_soft, v_soft)


def solution(mesh):
    n, zn = mesh.shape["ctx"], mesh.shape["head"]
    return jax.shard_map(
        functools.partial(local, n, zn),
        mesh=mesh,
        in_specs=(
            P("ctx", "head"), P("ctx", "head"), P("ctx", "head"), P("ctx", "head"),
            P("head"), P("ctx", "head"), P("ctx", None), P("ctx", None),
        ),
        out_specs=(P("ctx", "head"), P("ctx", "head")),
        check_vma=False,
    )
```

time: 230 us -> 47.8 us (0.21)
  the two profiles are of different devices: /device:TPU:6 before, /device:TPU:23 now
where the time goes in v1:
time: 47.8 us; the launch traced here: 46.9 us
  Pallas kernels  41.5 us (87%)
  local copies, waits for them, and re-layouts  4.84 us (10%)
  between operations  0.65 us (1%)
    pallas_call x1, Pallas kernels, local(): pl.pallas_call(functools.partial(kernel, n, zn, heads, kvc, ch), out_shap...  41.5 us
    unnamed x5, local copies, waits for them, and re-layouts  4.84 us

profile of v1, /device:TPU:23, one launch (start us, length us, event | category | flops | bytes accessed | tf_op | source)
XLA Modules:
  0.0 46.9 jit_solution(10334326795630001861)
XLA Ops:
  0.6 1.5 %copy.10.ld_ref = f32[256,16]{1,0:T(8,128)} copy(f32[256,16]{0,1:T(8,128)} %param.11) | data formatting | bytes 32768 | tf_op args[3]
  2.1 41.5 %shard_map.95 = (bf16[256,2048]{1,0:T(8,128)(2,1)}, bf16[256,2048]{1,0:T(8,128)(2,1)}) custom-call(f32[256,16]{1,0:T(8,128)} %copy.10.ld_ref, f32[16,128]{1,0:T(8,128)} %bitcast.1, bf16[256,2048]{1,0:T(8,128)(2,1)} %ql_hbm.1, bf16[256,2048]{1,0:T(8,128)(2,1)} %kl_hbm.1, bf16[256,2048]{1,0:T(8,128)(2,1)} %vl_hbm.1, bf16[256,2048]{1,0:T(8,128)(2,1)} %qs_hbm.1, ...), custom_call_target="tpu_custom_call" | custom-call | tf_op jit(solution)/shard_map/pallas_call | solution.py:359
  43.6 0.0 copy-start
  43.6 2.4 %copy.13 = bf16[256,2048]{1,0:T(8,128)(2,1)} copy(bf16[256,2048]{1,0:T(8,128)(2,1)} %get-tuple-element.4) | data formatting | bytes 2097152
  46.0 0.0 copy-done
  46.0 1.0 %copy.14 = bf16[256,2048]{1,0:T(8,128)(2,1)} copy(bf16[256,2048]{1,0:T(8,128)(2,1)S(1)} %copy-done) | data formatting | bytes 2097152
Async XLA Ops:
  43.6 2.4 %copy-start = (bf16[256,2048]{1,0:T(8,128)(2,1)S(1)}, bf16[256,2048]{1,0:T(8,128)(2,1)}, u32[]{:S(2)}) copy-start(bf16[256,2048]{1,0:T(8,128)(2,1)} %get-tuple-element.5) | copy-start | bytes 3145732

commit v2 on v1

--- a/solution.py
+++ b/solution.py
@@ -12,6 +12,8 @@
 KV_HEADS = 8
 EPSILON = 1e-06
 NEGATIVE = -1e30
+OWN_HEADS = 8
+FULL_HEADS = 8
 LOG2E = 1.4426950408889634
 MESH = pl.DeviceIdType.MESH
 F32 = jnp.float32
@@ -33,7 +35,7 @@
     n, zn, heads, kvc, ch,
     ld_ref, gain_ref, ql_hbm, kl_hbm, vl_hbm, qs_hbm, ks_hbm, vs_hbm,
     lin_hbm, soft_hbm,
-    ql, kl, vl, qs, kv, lin, soft, cumc, cumr, state, mixed, ein, eout, mx, tot, acc, pw,
+    ql, kl, vl, qs, kt, vv, kown, lin, soft, cumc, cumr, state, mixed, ein, eout, mx, tot, acc, pw,
     in_sem, own_sem, out_sem, kv_recv, dir_send, sib_send, rel_send, ch_send, ch_recv, pw_send, pw_recv,
 ):
     c = lax.axis_index("ctx")
@@ -47,9 +49,10 @@
 
     start = pl.multiple_of((z * heads // (QUERY_HEADS // KV_HEADS)) * DH, DH)
     own = [
-        pltpu.make_async_copy(src.at[:, pl.ds(start, kvc * DH)], kv.at[c, i], own_sem.at[i])
-        for i, src in enumerate((ks_hbm, vs_hbm))
+        pltpu.make_async_copy(src.at[:, pl.ds(start, kvc * DH)], dst, own_sem.at[i])
+        for i, (src, dst) in enumerate(((ks_hbm, kown), (vs_hbm, vv.at[c])))
     ]
+    places = (kt, vv)
     loads = [
         pltpu.make_async_copy(src, dst, in_sem.at[i])
         for i, (src, dst) in enumerate(((kl_hbm, kl), (vl_hbm, vl), (ql_hbm, ql), (qs_hbm, qs)))
@@ -66,7 +69,7 @@
 
     def kv_copy(block, i, send, target):
         return pltpu.make_async_remote_copy(
-            src_ref=kv.at[block, i], dst_ref=kv.at[block, i],
+            src_ref=places[i].at[block], dst_ref=places[i].at[block],
             send_sem=send, recv_sem=kv_recv.at[block, i],
             device_id={"ctx": target}, device_id_type=MESH,
         )
@@ -85,6 +88,7 @@
 
     for copy in own:
         copy.wait()
+    kt[c] = kown[...].astype(F32).T.astype(BF16)
 
     @pl.when(core == 0)
     def _():
@@ -96,14 +100,18 @@
             direct(i, to).start()
         return 0
 
-    lax.fori_loop(chip + 1, chips, send_direct, 0)
+    near = jnp.minimum(chip + 3, chips)
+    lax.fori_loop(chip + 1, near, send_direct, 0)
+
+    def send_far():
+        lax.fori_loop(near, chips, send_direct, 0)
 
     row_id = lax.broadcasted_iota(jnp.int32, (rows, rows), 0)
     col_id = lax.broadcasted_iota(jnp.int32, (rows, rows), 1)
     tri = jnp.where(col_id <= row_id, 1.0, 0.0).astype(F32)
-    ld = ld_ref[...]
-    cum = mm(tri, ld, 1, 0, HIGHEST)
-    cumr[...] = cum.T
+    running = mm(ld_ref[...], tri, 1, 1, HIGHEST)
+    cumr[...] = running
+    cum = running.T
     for h in range(heads):
         cumc[h] = jnp.broadcast_to(cum[:, h : h + 1], (rows, DH))
     for copy in loads[:2]:
@@ -113,14 +121,19 @@
         cc = cumc[h]
         last = cc[rows - 1 : rows, :]
         decayed = (kl[:, cols(h)].astype(F32) * jnp.exp(last - cc)).astype(BF16)
-        state[h] = mm(decayed, vl[:, cols(h)], 0, 0)
-
-    def over_heads(body, count, unroll):
+        return [(state, mm(decayed, vl[:, cols(h)], 0, 0))]
+
+    def over_heads(body, count, unroll, base=0):
         unroll = min(unroll, count)
 
         def step(j, _):
-            for u in range(unroll):
-                body(j * unroll + u)
+            made = [(base + j * unroll + u, body(base + j * unroll + u)) for u in range(unroll)]
+            for h, results in made:
+                for ref, value in results:
+                    if ref is soft or ref is lin:
+                        ref[:, cols(h)] = value
+                    else:
+                        ref[h] = value
             return 0
 
         lax.fori_loop(0, count // unroll, step, 0)
@@ -130,13 +143,19 @@
         copy.wait()
 
     def intra(h):
-        raw = mm(ql[:, cols(h)], kl[:, cols(h)], 1, 1)
-        cc = cumc[h]
-        gap = jnp.concatenate([cc] * (rows // DH), axis=1) - cumr[pl.ds(h, 1), :]
-        r = lax.broadcasted_iota(jnp.int32, (rows, rows), 0)
-        s = lax.broadcasted_iota(jnp.int32, (rows, rows), 1)
-        w = (raw * jnp.exp(jnp.where(s <= r, gap, NEGATIVE))).astype(BF16)
-        mixed[h] = mm(w, vl[:, cols(h)], 1, 0)
+        q, k, v, cc = ql[:, cols(h)], kl[:, cols(h)], vl[:, cols(h)], cumc[h]
+        across = cumr[pl.ds(h, 1), :]
+        half = rows // 2
+        parts = []
+        for low in (0, half):
+            high = low + half
+            raw = mm(q[low:high], k[:high], 1, 1)
+            gap = jnp.concatenate([cc[low:high]] * (high // DH), axis=1) - across[:, :high]
+            r = lax.broadcasted_iota(jnp.int32, (half, high), 0) + low
+            t = lax.broadcasted_iota(jnp.int32, (half, high), 1)
+            w = (raw * jnp.exp(jnp.where(t <= r, gap, NEGATIVE))).astype(BF16)
+            parts.append(mm(w, v[:high], 1, 0))
+        return [(mixed, jnp.concatenate(parts, axis=0))]
 
     def chain_copy(j):
         return pltpu.make_async_remote_copy(
@@ -160,16 +179,28 @@
 
             @pl.when(c < n - 1)
             def _():
+                leaving = []
                 for u in range(ch):
                     h = j * ch + u
                     fade = jnp.exp(cumc[h, rows - 1 : rows, :])
-                    eout[h] = (fade * ein[h].astype(F32) + state[h]).astype(BF16)
+                    leaving.append((fade * ein[h].astype(F32) + state[h]).astype(BF16))
+                for u in range(ch):
+                    eout[j * ch + u] = leaving[u]
                 chain_copy(j).start()
 
+            return 0
+
+        lax.fori_loop(0, chunks, step, 0)
+
+    def carry():
+        def step(j, _):
+            made = []
             for u in range(ch):
                 h = j * ch + u
                 carried = mm(ql[:, cols(h)], ein[h], 1, 0)
-                mixed[h] = mixed[h] + carried * jnp.exp(cumc[h])
+                made.append(mixed[h] + carried * jnp.exp(cumc[h]))
+            for u in range(ch):
+                mixed[j * ch + u] = made[u]
             return 0
 
         lax.fori_loop(0, chunks, step, 0)
@@ -193,47 +224,46 @@
 
     scale = DH ** (-0.5) * LOG2E
 
-    def group_dot(h, keys):
-        return mm(qs[:, cols(h)], keys, 1, 1) * scale
-
     def soft_own():
         for g in range(kvc):
-            keys = kv[c, 0, :, g * DH : (g + 1) * DH]
-            values = kv[c, 1, :, g * DH : (g + 1) * DH]
-
-            def one(u):
-                h = g * group + u
-                s = group_dot(h, keys)
+            part = slice(g * DH, (g + 1) * DH)
+            keys = kt[c, part, :]
+            values = vv[c, :, part]
+
+            def one(h):
+                s = mm(qs[:, cols(h)], keys, 1, 0) * scale
                 r = lax.broadcasted_iota(jnp.int32, (rows, rows), 0)
                 t = lax.broadcasted_iota(jnp.int32, (rows, rows), 1)
                 s = jnp.where(t <= r, s, NEGATIVE)
-                top = jnp.max(s, axis=1, keepdims=True)
-                p = jnp.exp2(s - top)
-                mx[h] = jnp.broadcast_to(top, (rows, DH))
-                tot[h] = sum(p[:, i : i + DH] for i in range(0, rows, DH))
-                acc[h] = mm(p.astype(BF16), values, 1, 0)
-
-            over_heads(one, group, 4)
+                top = jnp.broadcast_to(jnp.max(s, axis=1, keepdims=True), (rows, DH))
+                p = [jnp.exp2(s[:, i : i + DH] - top) for i in range(0, rows, DH)]
+                packed = jnp.concatenate([x.astype(BF16) for x in p], axis=1)
+                return [(mx, top), (tot, sum(p)), (acc, mm(packed, values, 1, 0))]
+
+            over_heads(one, group, OWN_HEADS, g * group)
 
     def soft_full(first, count):
         for g in range(kvc):
             part = slice(g * DH, (g + 1) * DH)
-            keys = kv[pl.ds(first, count), 0, :, part].reshape(count * rows, DH)
-            values = kv[pl.ds(first, count), 1, :, part].reshape(count * rows, DH)
-
-            def one(u):
-                h = g * group + u
-                s = group_dot(h, keys)
+            keys = [kt[first + b, part, :] for b in range(count)]
+            values = vv[pl.ds(first, count), :, part].reshape(count * rows, DH)
+
+            def one(h):
+                q = qs[:, cols(h)]
+                s = [mm(q, k, 1, 0) * scale for k in keys]
                 before = mx[h]
-                top = jnp.maximum(before, jnp.max(s, axis=1, keepdims=True))
+                high = functools.reduce(jnp.maximum, s)
+                top = jnp.maximum(before, jnp.max(high, axis=1, keepdims=True))
                 fade = jnp.exp2(before - top)
-                p = [jnp.exp2(s[:, i : i + DH] - top) for i in range(0, count * rows, DH)]
-                mx[h] = top
-                tot[h] = tot[h] * fade + sum(p)
+                p = [jnp.exp2(x[:, i : i + DH] - top) for x in s for i in range(0, rows, DH)]
                 packed = jnp.concatenate([x.astype(BF16) for x in p], axis=1)
-                acc[h] = acc[h] * fade + mm(packed, values, 1, 0)
-
-            over_heads(one, group, 4)
+                return [
+                    (mx, top),
+                    (tot, tot[h] * fade + sum(p)),
+                    (acc, acc[h] * fade + mm(packed, values, 1, 0)),
+                ]
+
+            over_heads(one, group, FULL_HEADS, g * group)
 
     def relay(source):
         for i in range(2):
@@ -249,19 +279,26 @@
     def _():
         first_chain()
 
-    over_heads(intra, heads, 2)
+    @pl.when(c == 1)
+    def _():
+        chain()
+
+    @pl.when(chip == 0)
+    def _():
+        send_far()
+
+    over_heads(intra, heads, 4)
 
     @pl.when(chip > 0)
     def _():
         relay(chip - 1)
 
-    @pl.when(c == 0)
-    def _():
-        power()
-
     @pl.when(c == 1)
     def _():
-        chain()
+        carry()
+
+    @pl.when(chip == 0)
+    def _():
         power()
 
     soft_own()
@@ -280,6 +317,8 @@
             @pl.when(source == 0)
             def _():
                 chain()
+                send_far()
+                carry()
                 power()
 
             @pl.when(source > 0)
@@ -292,10 +331,9 @@
         lax.fori_loop(0, chip, step, 0)
 
     def soft_end(h):
-        total = jnp.sum(tot[h], axis=1, keepdims=True)
-        soft[:, cols(h)] = (acc[h] / total).astype(BF16)
-
-    over_heads(soft_end, heads, 2)
+        return [(soft, (acc[h] / jnp.sum(tot[h], axis=1, keepdims=True)).astype(BF16))]
+
+    over_heads(soft_end, heads, 4)
     soft_out = pltpu.make_async_copy(soft, soft_hbm, out_sem.at[0])
     soft_out.start()
 
@@ -308,9 +346,9 @@
     norm = lax.rsqrt(mean + EPSILON)
 
     def lin_end(h):
-        lin[:, cols(h)] = (mixed[h] * norm * gain_ref[pl.ds(h, 1), :]).astype(BF16)
-
-    over_heads(lin_end, heads, 2)
+        return [(lin, (mixed[h] * norm * gain_ref[pl.ds(h, 1), :]).astype(BF16))]
+
+    over_heads(lin_end, heads, 4)
     lin_out = pltpu.make_async_copy(lin, lin_hbm, out_sem.at[1])
     lin_out.start()
 
@@ -363,7 +401,9 @@
         out_specs=(anywhere, anywhere),
         scratch_shapes=[
             wide, wide, wide, wide,
-            pltpu.VMEM((n, 2, rows, kvc * DH), BF16),
+            pltpu.VMEM((n, kvc * DH, rows), BF16),
+            pltpu.VMEM((n, rows, kvc * DH), BF16),
+            pltpu.VMEM((rows, kvc * DH), BF16),
             wide, wide,
             per_head,
             pltpu.VMEM((heads, rows), F32),
@@ -380,7 +420,7 @@
         compiler_params=pltpu.CompilerParams(
             collective_id=0, has_side_effects=True, vmem_limit_bytes=56 * 2**20
         ),
-    )(log_decay, norm_gain.reshape(heads, DH), q_linear, k_linear, v_linear, q_soft, k_soft, v_soft)
+    )(log_decay.T, norm_gain.reshape(heads, DH), q_linear, k_linear, v_linear, q_soft, k_soft, v_soft)
 
 
 def solution(mesh):

time: 47.8 us -> 47.1 us (0.985); the launches traced: 46.9 us -> 46.9 us
  local copies, waits for them, and re-layouts: 4.84 us -> 3.37 us
  Pallas kernels: 41.5 us -> 42.8 us
    unnamed x5 -> x4, local copies, waits for them, and re-layouts: 4.84 us -> 3.37 us
    pallas_call x1, Pallas kernels: 41.5 us -> 42.8 us  [local(): pl.pallas_call(functools.partial(kernel, n, zn, heads, kvc, ch), out_shap...]
where the time goes in v2:
time: 47.1 us; the launch traced here: 46.9 us
  Pallas kernels  42.8 us (91%)
  local copies, waits for them, and re-layouts  3.37 us (7%)
  between operations  0.65 us (1%)
    pallas_call x1, Pallas kernels, local(): pl.pallas_call(functools.partial(kernel, n, zn, heads, kvc, ch), out_shap...  42.8 us
    unnamed x4, local copies, waits for them, and re-layouts  3.37 us

profile of v2, /device:TPU:23, one launch (start us, length us, event | category | flops | bytes accessed | tf_op | source)
XLA Modules:
  0.0 46.9 jit_solution(14241180923058572724)
XLA Ops:
  0.6 42.8 %shard_map.95 = (bf16[256,2048]{1,0:T(8,128)(2,1)}, bf16[256,2048]{1,0:T(8,128)(2,1)}) custom-call(f32[16,256]{1,0:T(8,128)} %bitcast.2, f32[16,128]{1,0:T(8,128)} %bitcast.3, bf16[256,2048]{1,0:T(8,128)(2,1)} %ql_hbm.1, bf16[256,2048]{1,0:T(8,128)(2,1)} %kl_hbm.1, bf16[256,2048]{1,0:T(8,128)(2,1)} %vl_hbm.1, bf16[256,2048]{1,0:T(8,128)(2,1)} %qs_hbm.1, ...), custom_call_target="tpu_custom_call" | custom-call | tf_op jit(solution)/shard_map/pallas_call | solution.py:397
  43.5 0.0 copy-start
  43.5 2.4 %copy.12 = bf16[256,2048]{1,0:T(8,128)(2,1)} copy(bf16[256,2048]{1,0:T(8,128)(2,1)} %get-tuple-element.4) | data formatting | bytes 2097152
  45.9 0.0 copy-done
  45.9 1.0 %copy.13 = bf16[256,2048]{1,0:T(8,128)(2,1)} copy(bf16[256,2048]{1,0:T(8,128)(2,1)S(1)} %copy-done) | data formatting | bytes 2097152
Async XLA Ops:
  43.5 2.4 %copy-start = (bf16[256,2048]{1,0:T(8,128)(2,1)S(1)}, bf16[256,2048]{1,0:T(8,128)(2,1)}, u32[]{:S(2)}) copy-start(bf16[256,2048]{1,0:T(8,128)(2,1)} %get-tuple-element.5) | copy-start | bytes 3145732

commit v3 on v2

--- a/solution.py
+++ b/solution.py
@@ -100,11 +100,7 @@
             direct(i, to).start()
         return 0
 
-    near = jnp.minimum(chip + 3, chips)
-    lax.fori_loop(chip + 1, near, send_direct, 0)
-
-    def send_far():
-        lax.fori_loop(near, chips, send_direct, 0)
+    lax.fori_loop(chip + 1, chips, send_direct, 0)
 
     row_id = lax.broadcasted_iota(jnp.int32, (rows, rows), 0)
     col_id = lax.broadcasted_iota(jnp.int32, (rows, rows), 1)
@@ -283,10 +279,6 @@
     def _():
         chain()
 
-    @pl.when(chip == 0)
-    def _():
-        send_far()
-
     over_heads(intra, heads, 4)
 
     @pl.when(chip > 0)
@@ -317,7 +309,6 @@
             @pl.when(source == 0)
             def _():
                 chain()
-                send_far()
                 carry()
                 power()
 

time: 47.1 us -> 46.3 us (0.983); the launches traced: 46.9 us -> 45.4 us
  Pallas kernels: 42.8 us -> 41.4 us
    pallas_call x1, Pallas kernels: 42.8 us -> 41.4 us  [local(): pl.pallas_call(functools.partial(kernel, n, zn, heads, kvc, ch), out_shap...]
where the time goes in v3:
time: 46.3 us; the launch traced here: 45.4 us
  Pallas kernels  41.4 us (89%)
  local copies, waits for them, and re-layouts  3.37 us (7%)
  between operations  0.65 us (1%)
    pallas_call x1, Pallas kernels, local(): pl.pallas_call(functools.partial(kernel, n, zn, heads, kvc, ch), out_shap...  41.4 us
    unnamed x4, local copies, waits for them, and re-layouts  3.37 us

profile of v3, /device:TPU:23, one launch (start us, length us, event | category | flops | bytes accessed | tf_op | source)
XLA Modules:
  0.0 45.4 jit_solution(7333916345284235985)
XLA Ops:
  0.6 41.4 %shard_map.95 = (bf16[256,2048]{1,0:T(8,128)(2,1)}, bf16[256,2048]{1,0:T(8,128)(2,1)}) custom-call(f32[16,256]{1,0:T(8,128)} %bitcast.2, f32[16,128]{1,0:T(8,128)} %bitcast.3, bf16[256,2048]{1,0:T(8,128)(2,1)} %ql_hbm.1, bf16[256,2048]{1,0:T(8,128)(2,1)} %kl_hbm.1, bf16[256,2048]{1,0:T(8,128)(2,1)} %vl_hbm.1, bf16[256,2048]{1,0:T(8,128)(2,1)} %qs_hbm.1, ...), custom_call_target="tpu_custom_call" | custom-call | tf_op jit(solution)/shard_map/pallas_call | solution.py:388
  42.1 0.0 copy-start
  42.1 2.4 %copy.12 = bf16[256,2048]{1,0:T(8,128)(2,1)} copy(bf16[256,2048]{1,0:T(8,128)(2,1)} %get-tuple-element.4) | data formatting | bytes 2097152
  44.5 0.0 copy-done
  44.5 1.0 %copy.13 = bf16[256,2048]{1,0:T(8,128)(2,1)} copy(bf16[256,2048]{1,0:T(8,128)(2,1)S(1)} %copy-done) | data formatting | bytes 2097152
Async XLA Ops:
  42.1 2.4 %copy-start = (bf16[256,2048]{1,0:T(8,128)(2,1)S(1)}, bf16[256,2048]{1,0:T(8,128)(2,1)}, u32[]{:S(2)}) copy-start(bf16[256,2048]{1,0:T(8,128)(2,1)} %get-tuple-element.5) | copy-start | bytes 3145732
